TPU v7x, 32 devices: a whole 2x2x4 slice. The times are simulated.
32 devices in a mesh: seq: 16 (over z, y, core), kv: 2 (over x).
Axes of the slice: x: 2, y: 2, z: 4, core: 2. Of those that a mesh axis runs over, the one named last changes fastest.
Arguments:
- plan: int32 [16], replicated, may hold values from 0 to 15, each once
- queries: bfloat16 [2048, 1024], P('seq', 'kv'), may hold values from -24 to 24
- keys: bfloat16 [2048, 256], P('seq', 'kv'), may hold values from -9 to 9
- student_c: bfloat16 [2048, 1024], P('seq', 'kv'), may hold values from -0.125 to 0.125
- layer_input: bfloat16 [2048, 8192], P('seq', 'kv'), may hold values from -6 to 6
- b_weight: bfloat16 [2, 8192, 128], P('kv'), may hold values from -0.0625 to 0.0625
Outputs:
- grad_c: bfloat16 [2048, 1024], P('seq', 'kv')
- grad_wb: float32 [2, 8192, 128], P('kv', 'seq')
Inputs may be any that keep to these rules, and one draw needn't show every extreme that they name: Each value appears once: plan[d] is the block of 128 consecutive positions held by index d of seq.
All inputs are finite; a program needn't handle non-finite values.
Results may differ from a plain program's by a relative error of at most 0.0049.
Values may be sent and summed in bfloat16 or wider, within the bound.
A program may use at most 64 MiB of HBM per device.

v0:
```python
import math
import jax
import jax.numpy as jnp
from jax import lax
from jax.sharding import PartitionSpec as P

NEG_FILL = -1e30


def block_sweep(update, running, pieces, shard_rows):
    total_rows = pieces[0].shape[0]
    shard_count = total_rows // shard_rows
    block_limit = max(1, 1024 // shard_rows)
    factor = 1
    for option in range(1, shard_count + 1):
        if shard_count % option == 0 and option <= block_limit:
            factor = option
    block_rows = factor * shard_rows
    block_count = total_rows // block_rows
    stacked = tuple(
        (member.reshape((block_count, block_rows) + member.shape[1:]) for member in pieces)
    )
    offsets = block_rows * jnp.arange(block_count, dtype=jnp.int32)

    def advance(partial_state, inputs):
        return (update(partial_state, inputs[0], inputs[1]), None)

    running, unused = lax.scan(advance, running, (stacked, offsets))
    return running


def local(plan, queries, keys, student_c, layer_input, b_weight):
    shard_rows = keys.shape[0]
    state_width = keys.shape[1]
    head_count = queries.shape[1] // state_width
    seq_count = lax.axis_size("seq")
    token_count = shard_rows * seq_count
    student_scale = 2.0 / math.sqrt(token_count)
    score_scale = 1.0 / math.sqrt(state_width)
    block_ids = jnp.arange(seq_count, dtype=jnp.int32)

    def positions_of(global_rows):
        owner_ids = global_rows // shard_rows
        picked = jnp.sum(
            jnp.where(owner_ids[:, None] == block_ids[None, :], plan[None, :], 0), axis=1
        )
        return picked * shard_rows + global_rows % shard_rows

    own_start = lax.axis_index("seq") * shard_rows
    query_pos = positions_of(own_start + jnp.arange(shard_rows, dtype=jnp.int32))
    query_heads = queries.reshape(shard_rows, head_count, state_width)
    student_heads = student_c.reshape(shard_rows, head_count, state_width)
    features = lax.all_gather(layer_input, "kv", axis=1, tiled=True)
    b_local = jnp.dot(features, b_weight[0], preferred_element_type=jnp.float32).astype(
        jnp.bfloat16
    )

    def scores_of(key_block, offset):
        key_pos = positions_of(offset + jnp.arange(key_block.shape[0], dtype=jnp.int32))
        visible = key_pos[None, None, :] <= query_pos[:, None, None]
        scores = (
            jnp.einsum("qhd,kd->qhk", query_heads, key_block, preferred_element_type=jnp.float32)
            * score_scale
        )
        return (jnp.where(visible, scores, NEG_FILL), visible)

    def stats_step(running, members, offset):
        highest, totals = running
        scores, visible = scores_of(members[0], offset)
        raised = jnp.maximum(highest, jnp.max(scores, axis=-1))
        weights = jnp.where(visible, jnp.exp(scores - raised[..., None]), 0.0)
        return (raised, totals * jnp.exp(highest - raised) + jnp.sum(weights, axis=-1))

    def pair_step(highest, totals):

        def advance_pair(running, members, offset):
            grad_acc, db_buffer = running
            key_block, b_block = members
            scores, visible = scores_of(key_block, offset)
            teacher = jnp.where(
                visible, jnp.exp(scores - highest[..., None]) / totals[..., None], 0.0
            )
            student = student_scale * jnp.einsum(
                "qhd,kd->qhk", student_heads, b_block, preferred_element_type=jnp.float32
            )
            residual = jnp.where(visible, student - teacher, 0.0).astype(jnp.bfloat16)
            grad_acc = grad_acc + jnp.einsum(
                "qhk,kd->qhd", residual, b_block, preferred_element_type=jnp.float32
            )
            contrib = jnp.einsum(
                "qhk,qhd->kd", residual, student_heads, preferred_element_type=jnp.float32
            )
            db_buffer = lax.dynamic_update_slice_in_dim(db_buffer, contrib, offset, 0)
            return (grad_acc, db_buffer)

        return advance_pair

    stats_init = (
        jnp.full((shard_rows, head_count), NEG_FILL, jnp.float32),
        jnp.zeros((shard_rows, head_count), jnp.float32),
    )
    pair_init = (
        jnp.zeros((shard_rows, head_count, state_width), jnp.float32),
        jnp.zeros((token_count, state_width), jnp.float32),
    )
    highest, totals = block_sweep(
        stats_step, stats_init, (lax.all_gather(keys, "seq", axis=0, tiled=True),), shard_rows
    )
    advance_pair = pair_step(highest, totals)
    grad_acc, db_buffer = block_sweep(
        advance_pair,
        pair_init,
        (
            lax.all_gather(keys, "seq", axis=0, tiled=True),
            lax.all_gather(b_local, "seq", axis=0, tiled=True),
        ),
        shard_rows,
    )
    arrived = lax.all_to_all(
        db_buffer.reshape(seq_count, shard_rows, state_width).astype(jnp.bfloat16),
        "seq",
        split_axis=0,
        concat_axis=0,
        tiled=True,
    ).astype(jnp.float32)
    b_grad = jnp.sum(arrived, axis=0).astype(jnp.bfloat16)
    weight_grad = lax.psum_scatter(
        jnp.einsum("td,tn->dn", features, b_grad, preferred_element_type=jnp.float32),
        "seq",
        scatter_dimension=0,
        tiled=True,
    )
    grad_c = grad_acc.reshape(shard_rows, head_count * state_width).astype(jnp.bfloat16)
    return (grad_c, weight_grad[None])


def solution(mesh):
    in_specs = (
        P(),
        P("seq", "kv"),
        P("seq", "kv"),
        P("seq", "kv"),
        P("seq", "kv"),
        P("kv", None, None),
    )
    out_specs = (P("seq", "kv"), P("kv", "seq", None))
    return jax.shard_map(local, mesh=mesh, in_specs=in_specs, out_specs=out_specs, check_vma=False)
```

profile of v0, /device:TPU:0, one launch (start us, length us, event | category | flops | bytes accessed | tf_op | source)
XLA Modules:
  0.0 205.9 jit_solution(17083190945803974519)
XLA Ops:
  9.3 26.4 %all_gather.12 = bf16[2048,128]{1,0:T(8,128)(2,1)} all-gather(bf16[128,128]{1,0:T(8,128)(2,1)} %param.12), channel_id=1, replica_groups=mesh['seq'=16,'kv'=2] {'seq'}, dimensions={0}, use_global_device_ids=true | all-gather | bytes 557056 | tf_op jit(solution)/shard_map/all_gather | solution.py:114
  37.7 15.4 %while.30 = (s32[]{:T(128)}, f32[128,4]{0,1:T(4,128)S(1)}, f32[128,4]{0,1:T(4,128)S(1)}, s32[2]{0:T(128)}, s32[16]{0:T(128)S(1)}, /*index=5*/s32[128]{0:T(128)S(...) while((s32[]{:T(128)}, f32[128,4]{0,1:T(4,128)S(1)}, ...), condition=%wide.region_5.6_spmd.clone, body=%wide.region_1.5_spmd.clone.sunk | while | flops 138624512 | bytes 5033156 | solution.py:28
  37.7 1.2 dynamic_slice.62
  40.5 2.8 %fusion.71 = (f32[128,4]{0,1:T(4,128)S(1)}, f32[1024,128,4]{1,0,2:T(8,128)}) fusion(pred[128,1024]{0,1:T(8,128)(4,1)S(1)} %broadcast_compare_fusion.4, bf16[128,4,128]{2,0,1:T(8,128)(2,1)} %get-tuple-element.599, bf16[2,1024,128]{2,1,0:T(8,128)(2,1)} %get-tuple-element.598, s32[]{:T(128)} %get-tuple-element.582), kind=kOutput, calls=%fused_computation.4.clone.1 | convolution fusion | flops 135790080 | bytes 2624000 | tf_op jit(solution)/shard_map/while/body/eval_jaxpr/qhd,kd->qhk/dot_general | solution.py:62
  43.3 2.1 %select_reduce_fusion.8 = f32[128,4]{0,1:T(4,128)S(1)} fusion(f32[1024,128,4]{1,0,2:T(8,128)} %get-tuple-element.559, f32[128,4]{0,1:T(4,128)S(1)} %select_maximum_fusion.2, pred[128,1024]{0,1:T(8,128)(4,1)S(1)} %broadcast_compare_fusion.4), kind=kLoop, calls=%fused_computation.3.clone.1 | loop fusion | flops 2620928 | bytes 2232320 | tf_op jit(solution)/shard_map/while/body/eval_jaxpr/reduce_sum | solution.py:72
  48.2 2.8 %fusion.71 = (f32[128,4]{0,1:T(4,128)S(1)}, f32[1024,128,4]{1,0,2:T(8,128)}) fusion(pred[128,1024]{0,1:T(8,128)(4,1)S(1)} %broadcast_compare_fusion.4, bf16[128,4,128]{2,0,1:T(8,128)(2,1)} %get-tuple-element.599, bf16[2,1024,128]{2,1,0:T(8,128)(2,1)} %get-tuple-element.598, s32[]{:T(128)} %get-tuple-element.582), kind=kOutput, calls=%fused_computation.4.clone.1 | convolution fusion | flops 135790080 | bytes 2624000 | tf_op jit(solution)/shard_map/while/body/eval_jaxpr/qhd,kd->qhk/dot_general | solution.py:62
  51.0 2.1 %select_reduce_fusion.8 = f32[128,4]{0,1:T(4,128)S(1)} fusion(f32[1024,128,4]{1,0,2:T(8,128)} %get-tuple-element.559, f32[128,4]{0,1:T(4,128)S(1)} %select_maximum_fusion.2, pred[128,1024]{0,1:T(8,128)(4,1)S(1)} %broadcast_compare_fusion.4), kind=kLoop, calls=%fused_computation.3.clone.1 | loop fusion | flops 2620928 | bytes 2232320 | tf_op jit(solution)/shard_map/while/body/eval_jaxpr/reduce_sum | solution.py:72
  53.2 2.3 %fusion.41 = bf16[128,128]{1,0:T(8,128)(2,1)S(1)} fusion(bf16[128,8192]{1,0:T(8,128)(2,1)} %all-gather.2.cloned.1.call-done, bf16[1,8192,128]{2,1,0:T(8,128)(2,1)S(1)} %copy-done), kind=kOutput, calls=%fused_computation.67 | convolution fusion | flops 268451840 | bytes 4227072 | tf_op jit(solution)/shard_map/dot_general | solution.py:54
  55.5 20.3 %all_gather.11 = bf16[2048,128]{1,0:T(8,128)(2,1)} all-gather(bf16[128,128]{1,0:T(8,128)(2,1)S(1)} %fusion.41), channel_id=1, replica_groups=mesh['seq'=16,'kv'=2] {'seq'}, dimensions={0}, use_global_device_ids=true | all-gather | bytes 557056 | tf_op jit(solution)/shard_map/all_gather | solution.py:115
  76.6 26.1 %while.31 = (s32[]{:T(128)}, f32[128,4,128]{2,0,1:T(8,128)}, bf16[2048,128]{1,0:T(8,128)(2,1)}, s32[2]{0:T(128)}, s32[16]{0:T(128)S(1)}, /*index=5*/s32[128]{0:T...) while((s32[]{:T(128)}, f32[128,4,128]{2,0,1:T(8,128)}, ...), condition=%wide.region_8.9_spmd.clone, body=%wide.region_6.8_spmd.clone.sunk | while | flops 541930496 | bytes 10123537 | solution.py:28
  76.6 1.3 dynamic_slice.66
  79.4 1.4 fusion.81
  80.8 2.0 fusion.83
  85.2 2.7 %dynamic_update_slice.8 = bf16[2048,128]{1,0:T(8,128)(2,1)} dynamic-update-slice(bf16[2048,128]{1,0:T(8,128)(2,1)} %get-tuple-element.619, bf16[1024,128]{1,0:T(8,128)(2,1)S(1)} %convolution_bitcast_fusion.3, s32[]{:T(128)S(6)} %select_n.206, s32[]{:T(128)} %constant.191.clone.1..sunk.1) | dynamic-update-slice | bytes 524292 | tf_op jit(solution)/shard_map/while/body/eval_jaxpr/dynamic_update_slice | solution.py:93
  87.9 2.1 %convolution_add_fusion.2 = f32[128,4,128]{2,0,1:T(8,128)} fusion(bf16[128,4,1024]{0,2,1:T(8,128)(2,1)S(1)} %fusion.83, f32[128,4,128]{2,0,1:T(8,128)} %get-tuple-element.618, bf16[2,1024,128]{2,1,0:T(8,128)(2,1)} %get-tuple-element.638, s32[]{:T(128)} %get-tuple-element.617, pred[]{:T(512)S(6)} %compare.39), kind=kOutput, calls=%fused_computation.37.clone.1 | convolution fusion | flops 134348800 | bytes 1835521 | tf_op jit(solution)/shard_map/while/body/eval_jaxpr/qhk,kd->qhd/dot_general | solution.py:87
  90.1 1.3 dynamic_slice.66
  92.9 1.4 fusion.81
  94.3 2.0 fusion.83
  98.7 1.8 dynamic_update_slice.8
  100.5 2.2 %convolution_add_fusion.2 = f32[128,4,128]{2,0,1:T(8,128)} fusion(bf16[128,4,1024]{0,2,1:T(8,128)(2,1)S(1)} %fusion.83, f32[128,4,128]{2,0,1:T(8,128)} %get-tuple-element.618, bf16[2,1024,128]{2,1,0:T(8,128)(2,1)} %get-tuple-element.638, s32[]{:T(128)} %get-tuple-element.617, pred[]{:T(512)S(6)} %compare.39), kind=kOutput, calls=%fused_computation.37.clone.1 | convolution fusion | flops 134348800 | bytes 1835521 | tf_op jit(solution)/shard_map/while/body/eval_jaxpr/qhk,kd->qhd/dot_general | solution.py:87
  102.7 18.0 %all_to_all.5 = bf16[16,128,128]{2,1,0:T(8,128)(2,1)S(1)} all-to-all(bf16[16,128,128]{2,1,0:T(8,128)(2,1)} %bitcast.107), channel_id=1, replica_groups=mesh['seq'=16,'kv'=2] {'seq'}, dimensions={0} | all-to-all | bytes 1048576 | tf_op jit(solution)/shard_map/all_to_all | solution.py:119
  120.8 4.2 %convolution_bitcast_fusion.1 = f32[8192,128]{0,1:T(8,128)} fusion(bf16[128,128]{1,0:T(8,128)(2,1)S(1)} %reduce_sum.58, bf16[128,8192]{1,0:T(8,128)(2,1)} %all-gather.2.cloned.1.call-done), kind=kOutput, calls=%fused_computation.64 | convolution fusion | flops 268435456 | bytes 6324224 | tf_op jit(solution)/shard_map/td,tn->dn/dot_general | solution.py:128
  126.6 70.7 %reduce-scatter.2.cloned.1.call-done = f32[512,128]{0,1:T(8,128)} async-done(((f32[8192,128]{0,1:T(8,128)}), f32[512,128]{0,1:T(8,128)}) %reduce-scatter.2.cloned.1.call-update) | async-done | bytes 262160 | tf_op jit(solution)/shard_map/reduce_scatter | solution.py:127
  197.3 1.8 copy.26
  (52 shorter events, 15.0 us)
Async XLA Ops:
  7.2 46.0 %copy-start = (bf16[1,8192,128]{2,1,0:T(8,128)(2,1)S(1)}, bf16[1,8192,128]{2,1,0:T(8,128)(2,1)}, u32[]{:S(2)}) copy-start(bf16[1,8192,128]{2,1,0:T(8,128)(2,1)} %param.15) | copy-start | bytes 6291460
  7.2 30.5 %copy-start.3 = (s32[16]{0:T(128)S(1)}, s32[16]{0:T(128)}, u32[]{:S(2)}) copy-start(s32[16]{0:T(128)} %param.10) | copy-start | bytes 196
  7.2 30.3 %copy-start.2 = (bf16[128,512]{1,0:T(8,128)(2,1)S(1)}, bf16[128,512]{1,0:T(8,128)(2,1)}, u32[]{:S(2)}) copy-start(bf16[128,512]{1,0:T(8,128)(2,1)} %param.13) | copy-start | bytes 393220
  7.2 45.9 %all-gather.2.cloned.1.call-start = ((), (), s32[]{:S(2)}) async-start(), calls=%async_computation.2 | async-start | bytes 3145728 | tf_op jit(solution)/shard_map/all_gather | solution.py:53
  7.9 189.4 %reduce-scatter.2.cloned.1.call-start = ((), (), s32[]{:S(2)}) async-start(), calls=%async_computation.3 | async-start | bytes 4456448 | tf_op jit(solution)/shard_map/reduce_scatter | solution.py:127
  125.0 0.9 copy-start.1
Sparse Core Ops, SparseCore 0:
  9.6 35.7 all-gather.1
  125.2 72.1 reduce-scatter.1
where the time goes:
time: 207 us; the launch traced here: 206 us
  waiting for transfers between devices  71.4 us (34%)
  blocking collectives  64.6 us (31%)
  matrix products  24.1 us (12%)
  local copies, waits for them, and re-layouts  15.1 us (7%)
  between operations  14.1 us (7%)
  other arithmetic  12.5 us (6%)
  loops' own time  4.02 us (2%)
    reduce_scatter x1, waiting for transfers between devices, local(): lax.psum_scatter(jnp.einsum('td,tn->dn', features, b_grad, preferred_elem...  70.7 us
    all_gather x1, blocking collectives, local(): lax.all_gather(keys, 'seq', axis=0, tiled=True)  26.4 us
    all_gather x1, blocking collectives, local(): lax.all_gather(b_local, 'seq', axis=0, tiled=True)  20.3 us
    all_to_all x1, blocking collectives, local(): lax.all_to_all(db_buffer.reshape(seq_count, shard_rows, state_width).asty...  18 us
    dot_general x4, matrix products, scores_of(): jnp.einsum('qhd,kd->qhk', query_heads, key_block, preferred_element_type=...  9.57 us
    dynamic_slice x4, local copies, waits for them, and re-layouts, block_sweep(): running, unused = lax.scan(advance, running, (stacked, offsets))  4.89 us
    unnamed x13, local copies, waits for them, and re-layouts  4.78 us
    dynamic_update_slice x2, local copies, waits for them, and re-layouts, advance_pair(): db_buffer = lax.dynamic_update_slice_in_dim(db_buffer, contrib, offset, 0)  4.53 us
  transfers between devices with their start and end apart: 2, of which 1 were waited for; matrix products, arithmetic and copies ran while one was open for 9% of the time, Pallas kernels for 0%

commit v1 on v0

--- a/solution.py
+++ b/solution.py
@@ -5,6 +5,28 @@
 from jax.sharding import PartitionSpec as P
 
 NEG_FILL = -1e30
+
+
+def array_plan(sample, join_dim):
+    sample = jnp.moveaxis(sample, 0, join_dim)
+    z_new = sample.shape
+    passed = sample.reshape(
+        *z_new[:join_dim], z_new[join_dim] * z_new[join_dim + 1], *z_new[join_dim + 2 :]
+    )
+    return passed
+
+
+def divide_sector(array_here, bus_axis):
+    f_now, low = (lax.axis_size(bus_axis), lax.axis_index(bus_axis))
+    block_out, small = (array_here[None], 1)
+    while small < f_now:
+        r2 = lax.ppermute(block_out, bus_axis, list(map(lambda d: (d, d ^ small), range(f_now))))
+        near = low & small == 0
+        block_out = jnp.concatenate(
+            [jnp.where(near, block_out, r2), jnp.where(near, r2, block_out)]
+        )
+        small *= 2
+    return block_out
 
 
 def block_sweep(update, running, pieces, shard_rows):
@@ -30,6 +52,12 @@
 
 
 def local(plan, queries, keys, student_c, layer_input, b_weight):
+
+    def carry_tables(raw, inp, k_dim):
+        z2 = divide_sector(raw, inp)
+        u1 = array_plan(z2, k_dim)
+        return u1
+
     shard_rows = keys.shape[0]
     state_width = keys.shape[1]
     head_count = queries.shape[1] // state_width
@@ -110,10 +138,7 @@
     grad_acc, db_buffer = block_sweep(
         advance_pair,
         pair_init,
-        (
-            lax.all_gather(keys, "seq", axis=0, tiled=True),
-            lax.all_gather(b_local, "seq", axis=0, tiled=True),
-        ),
+        (carry_tables(keys, "seq", 0), lax.all_gather(b_local, "seq", axis=0, tiled=True)),
         shard_rows,
     )
     arrived = lax.all_to_all(

time: 207 us -> 217 us (1.048)
  waiting for transfers between devices: 71.4 us -> 77.6 us
  other arithmetic: 12.5 us -> 15.9 us
    ppermute x0 -> x4, waiting for transfers between devices: none -> 7.11 us  [divide_sector(): lax.ppermute(block_out, bus_axis, list(map(lambda d: (d, d ^ small), rang...]
    all_gather x1, blocking collectives: 20.3 us -> 22.5 us  [local(): lax.all_gather(b_local, 'seq', axis=0, tiled=True)]
    unnamed x13 -> x15, local copies, waits for them, and re-layouts: 4.78 us -> 4.78 us
  transfers between devices with their start and end apart: 2 -> 6, of which waited for: 1 -> 3; matrix products, arithmetic and copies ran while one was open for 9% -> 11% of each run, Pallas kernels for 0% -> 0%
where the time goes in v1:
time: 217 us; the launch traced here: 216 us
  waiting for transfers between devices  77.6 us (36%)
  blocking collectives  65.3 us (30%)
  matrix products  23.8 us (11%)
  other arithmetic  15.9 us (7%)
  local copies, waits for them, and re-layouts  15.2 us (7%)
  between operations  14.2 us (7%)
  loops' own time  3.45 us (2%)
    reduce_scatter x1, waiting for transfers between devices, local(): lax.psum_scatter(jnp.einsum('td,tn->dn', features, b_grad, preferred_elem...  70.3 us
    all_gather x1, blocking collectives, local(): lax.all_gather(keys, 'seq', axis=0, tiled=True)  24.8 us
    all_gather x1, blocking collectives, local(): lax.all_gather(b_local, 'seq', axis=0, tiled=True)  22.5 us
    all_to_all x1, blocking collectives, local(): lax.all_to_all(db_buffer.reshape(seq_count, shard_rows, state_width).asty...  18 us
    dot_general x4, matrix products, scores_of(): jnp.einsum('qhd,kd->qhk', query_heads, key_block, preferred_element_type=...  9.25 us
    ppermute x4, waiting for transfers between devices, divide_sector(): lax.ppermute(block_out, bus_axis, list(map(lambda d: (d, d ^ small), rang...  7.11 us
    dynamic_slice x4, local copies, waits for them, and re-layouts, block_sweep(): running, unused = lax.scan(advance, running, (stacked, offsets))  5.04 us
    unnamed x15, local copies, waits for them, and re-layouts  4.78 us
  transfers between devices with their start and end apart: 6, of which 3 were waited for; matrix products, arithmetic and copies ran while one was open for 11% of the time, Pallas kernels for 0%

profile of v1, /device:TPU:0, one launch (start us, length us, event | category | flops | bytes accessed | tf_op | source)
XLA Modules:
  0.0 216.3 jit_solution(10526204895149403873)
XLA Ops:
  8.0 24.8 %all_gather.11 = bf16[2048,128]{1,0:T(8,128)(2,1)S(1)} all-gather(bf16[128,128]{1,0:T(8,128)(2,1)} %param.12), channel_id=1, replica_groups=mesh['seq'=16,'kv'=2] {'seq'}, dimensions={0}, use_global_device_ids=true | all-gather | bytes 557056 | tf_op jit(solution)/shard_map/all_gather | solution.py:135
  34.4 3.6 %collective-permute-done.1 = bf16[2,128,128]{2,1,0:T(8,128)(2,1)S(1)} collective-permute-done((bf16[2,128,128]{2,1,0:T(8,128)(2,1)S(1)}, bf16[2,128,128]{2,1,0:T(8,128)(2,1)S(1)}, u32[]{:S(2)}, u32[]{:S(2)}) %collective-permute-start.1) | collective-permute-done | bytes 65568 | tf_op jit(solution)/shard_map/ppermute | solution.py:23
  39.6 3.5 %collective-permute-done.2 = bf16[4,128,128]{2,1,0:T(8,128)(2,1)S(1)} collective-permute-done((bf16[4,128,128]{2,1,0:T(8,128)(2,1)S(1)}, bf16[4,128,128]{2,1,0:T(8,128)(2,1)S(1)}, u32[]{:S(2)}, u32[]{:S(2)}) %collective-permute-start.2) | collective-permute-done | bytes 131104 | tf_op jit(solution)/shard_map/ppermute | solution.py:23
  43.3 17.2 %while.30 = (s32[]{:T(128)}, f32[128,4]{0,1:T(4,128)S(1)}, f32[128,4]{0,1:T(4,128)}, s32[2]{0:T(128)}, s32[16]{0:T(128)S(1)}, /*index=5*/s32[128]{0:T(128)S(1)},...) while((s32[]{:T(128)}, f32[128,4]{0,1:T(4,128)S(1)}, ...), condition=%wide.region_5.6_spmd.clone, body=%wide.region_1.5_spmd.clone.sunk | while | flops 138624512 | bytes 5032648 | solution.py:50
  46.1 2.7 %fusion.71 = (f32[128,4]{0,1:T(4,128)S(1)}, f32[1024,128,4]{1,0,2:T(8,128)}) fusion(pred[128,1024]{0,1:T(8,128)(4,1)S(1)} %broadcast_compare_fusion.4, bf16[128,4,128]{2,0,1:T(8,128)(2,1)} %get-tuple-element.607, bf16[2,1024,128]{2,1,0:T(8,128)(2,1)S(1)} %get-tuple-element.606, s32[]{:T(128)} %get-tuple-element.590), kind=kOutput, calls=%fused_computation.4.clone.1 | convolution fusion | flops 135790080 | bytes 2623492 | tf_op jit(solution)/shard_map/while/body/eval_jaxpr/qhd,kd->qhk/dot_general | solution.py:90
  48.8 2.1 select_reduce_fusion.8
  54.4 2.7 %fusion.71 = (f32[128,4]{0,1:T(4,128)S(1)}, f32[1024,128,4]{1,0,2:T(8,128)}) fusion(pred[128,1024]{0,1:T(8,128)(4,1)S(1)} %broadcast_compare_fusion.4, bf16[128,4,128]{2,0,1:T(8,128)(2,1)} %get-tuple-element.607, bf16[2,1024,128]{2,1,0:T(8,128)(2,1)S(1)} %get-tuple-element.606, s32[]{:T(128)} %get-tuple-element.590), kind=kOutput, calls=%fused_computation.4.clone.1 | convolution fusion | flops 135790080 | bytes 2623492 | tf_op jit(solution)/shard_map/while/body/eval_jaxpr/qhd,kd->qhk/dot_general | solution.py:90
  57.1 2.1 select_reduce_fusion.8
  59.2 1.3 fusion.72
  62.6 2.3 %fusion.41 = bf16[128,128]{1,0:T(8,128)(2,1)S(1)} fusion(bf16[128,8192]{1,0:T(8,128)(2,1)} %all-gather.2.cloned.1.call-done, bf16[1,8192,128]{2,1,0:T(8,128)(2,1)S(1)} %copy-done), kind=kOutput, calls=%fused_computation.67 | convolution fusion | flops 268451840 | bytes 4227072 | tf_op jit(solution)/shard_map/dot_general | solution.py:82
  64.9 22.5 %all_gather.10 = bf16[2048,128]{1,0:T(8,128)(2,1)} all-gather(bf16[128,128]{1,0:T(8,128)(2,1)S(1)} %fusion.41), channel_id=1, replica_groups=mesh['seq'=16,'kv'=2] {'seq'}, dimensions={0}, use_global_device_ids=true | all-gather | bytes 557056 | tf_op jit(solution)/shard_map/all_gather | solution.py:141
  88.2 25.1 %while.31 = (s32[]{:T(128)}, f32[128,4,128]{2,0,1:T(8,128)}, bf16[2048,128]{1,0:T(8,128)(2,1)}, s32[2]{0:T(128)}, s32[16]{0:T(128)S(1)}, /*index=5*/s32[128]{0:T...) while((s32[]{:T(128)}, f32[128,4,128]{2,0,1:T(8,128)}, ...), condition=%wide.region_8.9_spmd.clone, body=%wide.region_6.8_spmd.clone.sunk | while | flops 541930496 | bytes 12220209 | solution.py:50
  90.9 1.4 fusion.81
  92.3 1.9 fusion.83
  96.3 2.7 %dynamic_update_slice.8 = bf16[2048,128]{1,0:T(8,128)(2,1)} dynamic-update-slice(bf16[2048,128]{1,0:T(8,128)(2,1)} %get-tuple-element.627, bf16[1024,128]{1,0:T(8,128)(2,1)S(1)} %convolution_bitcast_fusion.3, s32[]{:T(128)S(6)} %select_n.282, s32[]{:T(128)} %constant.195.clone.1..sunk.1) | dynamic-update-slice | bytes 524292 | tf_op jit(solution)/shard_map/while/body/eval_jaxpr/dynamic_update_slice | solution.py:121
  99.1 2.1 convolution_add_fusion.2
  103.9 1.4 fusion.81
  105.3 1.9 fusion.83
  109.3 1.8 dynamic_update_slice.8
  111.1 2.2 %convolution_add_fusion.2 = f32[128,4,128]{2,0,1:T(8,128)} fusion(bf16[128,4,1024]{0,2,1:T(8,128)(2,1)S(1)} %fusion.83, f32[128,4,128]{2,0,1:T(8,128)} %get-tuple-element.626, bf16[2,1024,128]{2,1,0:T(8,128)(2,1)} %get-tuple-element.646, s32[]{:T(128)} %get-tuple-element.625, pred[]{:T(512)S(6)} %compare.39), kind=kOutput, calls=%fused_computation.37.clone.1 | convolution fusion | flops 134348800 | bytes 1835521 | tf_op jit(solution)/shard_map/while/body/eval_jaxpr/qhk,kd->qhd/dot_general | solution.py:115
  113.3 18.0 %all_to_all.5 = bf16[16,128,128]{2,1,0:T(8,128)(2,1)S(1)} all-to-all(bf16[16,128,128]{2,1,0:T(8,128)(2,1)} %bitcast.112), channel_id=1, replica_groups=mesh['seq'=16,'kv'=2] {'seq'}, dimensions={0} | all-to-all | bytes 1048576 | tf_op jit(solution)/shard_map/all_to_all | solution.py:144
  131.4 4.3 %convolution_bitcast_fusion.1 = f32[8192,128]{0,1:T(8,128)} fusion(bf16[128,128]{1,0:T(8,128)(2,1)S(1)} %reduce_sum.58, bf16[128,8192]{1,0:T(8,128)(2,1)} %all-gather.2.cloned.1.call-done), kind=kOutput, calls=%fused_computation.64 | convolution fusion | flops 268435456 | bytes 6324224 | tf_op jit(solution)/shard_map/td,tn->dn/dot_general | solution.py:153
  137.3 70.3 %reduce-scatter.2.cloned.1.call-done = f32[512,128]{0,1:T(8,128)} async-done(((f32[8192,128]{0,1:T(8,128)}), f32[512,128]{0,1:T(8,128)}) %reduce-scatter.2.cloned.1.call-update) | async-done | bytes 262160 | tf_op jit(solution)/shard_map/reduce_scatter | solution.py:152
  207.6 1.8 copy.26
  (74 shorter events, 21.1 us)
Async XLA Ops:
  7.2 55.4 %copy-start = (bf16[1,8192,128]{2,1,0:T(8,128)(2,1)S(1)}, bf16[1,8192,128]{2,1,0:T(8,128)(2,1)}, u32[]{:S(2)}) copy-start(bf16[1,8192,128]{2,1,0:T(8,128)(2,1)} %param.15) | copy-start | bytes 6291460
  7.2 36.1 %copy-start.4 = (s32[16]{0:T(128)S(1)}, s32[16]{0:T(128)}, u32[]{:S(2)}) copy-start(s32[16]{0:T(128)} %param.10) | copy-start | bytes 196
  7.2 31.0 %copy-start.3 = (bf16[128,512]{1,0:T(8,128)(2,1)S(1)}, bf16[128,512]{1,0:T(8,128)(2,1)}, u32[]{:S(2)}) copy-start(bf16[128,512]{1,0:T(8,128)(2,1)} %param.11) | copy-start | bytes 393220
  7.2 55.4 %all-gather.2.cloned.1.call-start = ((), (), s32[]{:S(2)}) async-start(), calls=%async_computation.2 | async-start | bytes 3145728 | tf_op jit(solution)/shard_map/all_gather | solution.py:81
  7.2 25.6 %collective-permute-start = (bf16[1,128,128]{2,1,0:T(8,128)(2,1)}, bf16[1,128,128]{2,1,0:T(8,128)(2,1)S(1)}, u32[]{:S(2)}, u32[]{:S(2)}) collective-permute-start(bf16[1,128,128]{2,1,0:T(8,128)(2,1)} %bitcast.117), channel_id=1, source_target_pairs={{0,2},{2,0},{4,6},{6,4},{8,10},{10,8},{12,14},{14,12},{16,18},{18,... | collective-permute-start | bytes 98312 | tf_op jit(solution)/shard_map/ppermute | solution.py:23
  7.9 199.7 %reduce-scatter.2.cloned.1.call-start = ((), (), s32[]{:S(2)}) async-start(), calls=%async_computation.3 | async-start | bytes 4456448 | tf_op jit(solution)/shard_map/reduce_scatter | solution.py:152
  33.6 4.4 %collective-permute-start.1 = (bf16[2,128,128]{2,1,0:T(8,128)(2,1)S(1)}, bf16[2,128,128]{2,1,0:T(8,128)(2,1)S(1)}, u32[]{:S(2)}, u32[]{:S(2)}) collective-permute-start(bf16[2,128,128]{2,1,0:T(8,128)(2,1)S(1)} %pad_maximum_fusion.3), channel_id=1, source_target_pairs={{0,4},{2,6},{4,0},{6,2},{8,12},{10,14},{12,8},{14,10},{16,20},{18,... | collective-permute-start | bytes 196616 | tf_op jit(solution)/shard_map/ppermute | solution.py:23
  38.0 5.1 %collective-permute-start.2 = (bf16[4,128,128]{2,1,0:T(8,128)(2,1)S(1)}, bf16[4,128,128]{2,1,0:T(8,128)(2,1)S(1)}, u32[]{:S(2)}, u32[]{:S(2)}) collective-permute-start(bf16[4,128,128]{2,1,0:T(8,128)(2,1)S(1)} %pad_maximum_fusion.2), channel_id=1, source_target_pairs={{0,8},{2,10},{4,12},{6,14},{8,0},{10,2},{12,4},{14,6},{16,24},{18,... | collective-permute-start | bytes 393224 | tf_op jit(solution)/shard_map/ppermute | solution.py:23
  43.2 18.4 %collective-permute-start.3 = (bf16[8,128,128]{2,1,0:T(8,128)(2,1)S(1)}, bf16[8,128,128]{2,1,0:T(8,128)(2,1)S(1)}, u32[]{:S(2)}, u32[]{:S(2)}) collective-permute-start(bf16[8,128,128]{2,1,0:T(8,128)(2,1)S(1)} %pad_maximum_fusion.1), channel_id=1, source_target_pairs={{0,16},{2,18},{4,20},{6,22},{8,24},{10,26},{12,28},{14,30},{16,0},... | collective-permute-start | bytes 786440 | tf_op jit(solution)/shard_map/ppermute | solution.py:23
  62.6 25.6 %copy-start.5 = (f32[128,4]{0,1:T(4,128)S(1)}, f32[128,4]{0,1:T(4,128)}, u32[]{:S(2)}) copy-start(f32[128,4]{0,1:T(4,128)} %get-tuple-element.621) | copy-start | bytes 6148
  88.2 4.1 %copy-start.2 = (bf16[2,1024,128]{2,1,0:T(8,128)(2,1)S(1)}, bf16[2,1024,128]{2,1,0:T(8,128)(2,1)}, u32[]{:S(2)}) copy-start(bf16[2,1024,128]{2,1,0:T(8,128)(2,1)} %get-tuple-element.648) | copy-start | bytes 1572868 | tf_op jit(solution)/shard_map/while
  101.2 4.1 %copy-start.2 = (bf16[2,1024,128]{2,1,0:T(8,128)(2,1)S(1)}, bf16[2,1024,128]{2,1,0:T(8,128)(2,1)}, u32[]{:S(2)}) copy-start(bf16[2,1024,128]{2,1,0:T(8,128)(2,1)} %get-tuple-element.648) | copy-start | bytes 1572868 | tf_op jit(solution)/shard_map/while
  135.7 0.9 copy-start.1
Sparse Core Ops, SparseCore 0:
  9.6 35.8 all-gather.1
  135.8 71.7 reduce-scatter.1
